TPU v7x, 32 devices: a whole 2x2x4 slice. The times are simulated.
32 devices in a mesh: dp: 8 (over z, x), feat: 4 (over y, core).
Axes of the slice: x: 2, y: 2, z: 4, core: 2. Of those that a mesh axis runs over, the one named last changes fastest.
Arguments:
- samples: bfloat16 [8192, 1024], P('dp', 'feat'), may hold values from -6 to 6
- freqs: bfloat16 [1024, 32768], P('dp', 'feat'), may hold values from -0.1875 to 0.1875
- phases: float32 [32768], P('feat'), may hold values from -3.140625 to 3.140625
- range_test: bfloat16 [32768, 256], P('feat'), may hold values from -6 to 6
- corange_test: bfloat16 [256, 8192], P(None, 'dp'), may hold values from -6 to 6
Outputs:
- range_sketch: float32 [8192, 256], P(('dp', 'feat'))
- corange_sketch: float32 [256, 32768], P('dp', 'feat')
All inputs are finite; a program needn't handle non-finite values.
Results may differ from a plain program's by a relative error of at most 0.0024.
Values may be sent and summed in bfloat16 or wider, within the bound.
A program may use at most 128 MiB of HBM per device.

v0:
```python
import math
import jax
import jax.numpy as jnp
from jax import lax
from jax.sharding import PartitionSpec as P


def on_device(samples, freqs, phases, range_test, corange_test):
    gathered = lax.all_gather(samples, "feat", axis=1, tiled=True)
    feature_count = freqs.shape[1]
    projection = jnp.dot(
        gathered,
        lax.all_gather(freqs, "dp", axis=0, tiled=True),
        preferred_element_type=jnp.float32,
    )
    scale = math.sqrt(2.0 / (feature_count * lax.axis_size("feat")))
    features = (scale * jnp.cos(projection + phases[None, :])).astype(jnp.bfloat16)
    range_sketch = lax.psum_scatter(
        jnp.dot(features, range_test, preferred_element_type=jnp.float32),
        "feat",
        scatter_dimension=0,
        tiled=True,
    )
    corange_sketch = lax.psum_scatter(
        jnp.dot(corange_test, features, preferred_element_type=jnp.float32),
        "dp",
        scatter_dimension=0,
        tiled=True,
    )
    return (range_sketch, corange_sketch)


def solution(mesh):
    placed = (P("dp", "feat"), P("dp", "feat"), P("feat"), P("feat", None), P(None, "dp"))
    return jax.shard_map(
        on_device,
        mesh=mesh,
        in_specs=placed,
        out_specs=(P(("dp", "feat"), None), P("dp", "feat")),
        check_vma=False,
    )
```

profile of v0, /device:TPU:0, one launch (start us, length us, event | category | flops | bytes accessed | tf_op | source)
XLA Modules:
  0.0 583.5 jit_solution(11586309907684146967)
XLA Ops:
  7.2 0.0 copy-start
  7.2 0.0 all-gather.3.cloned.1.call-start
  7.2 0.7 all-gather.3.cloned.1.call-update
  7.9 0.0 all-gather.5.cloned.1.call-start
  8.0 0.7 all-gather.5.cloned.1.call-update
  8.7 0.0 reduce-scatter.5.cloned.1.call-start
  8.7 26.4 %all-gather.3.cloned.1.call-done = bf16[1024,1024]{1,0:T(8,128)(2,1)} async-done(((bf16[1024,256]{1,0:T(8,128)(2,1)}), bf16[1024,1024]{1,0:T(8,128)(2,1)}) %all-gather.3.cloned.1.call-update) | async-done | bytes 2097168 | tf_op jit(solution)/shard_map/all_gather | solution.py:9
  35.1 229.8 %all-gather.5.cloned.1.call-done = bf16[1024,8192]{1,0:T(8,128)(2,1)} async-done(((bf16[128,8192]{1,0:T(8,128)(2,1)}), bf16[1024,8192]{1,0:T(8,128)(2,1)}) %all-gather.5.cloned.1.call-update) | async-done | bytes 16777232 | tf_op jit(solution)/shard_map/all_gather | solution.py:13
  264.9 0.0 copy-start.1
  264.9 124.0 %multiply_convert_fusion = bf16[1024,8192]{1,0:T(8,128)(2,1)S(1)} fusion(bf16[1024,1024]{1,0:T(8,128)(2,1)} %all-gather.3.cloned.1.call-done, bf16[1024,8192]{1,0:T(8,128)(2,1)} %all-gather.5.cloned.1.call-done, f32[8192]{0:T(1024)} %param.7), kind=kOutput, calls=%fused_computation | convolution fusion | flops 17205035008 | bytes 35684352 | tf_op jit(solution)/shard_map/dot_general | solution.py:11
  388.9 0.0 copy-start.2
  388.9 5.7 copy-done.2
  394.6 0.0 copy-done.1
  394.6 5.5 fusion
  400.2 0.0 reduce-scatter.5.cloned.1.call-update
  400.2 0.0 reduce-scatter.7.cloned.1.call-start
  400.2 0.0 copy-done
  400.3 14.1 %convolution_bitcast_fusion = f32[256,8192]{0,1:T(8,128)} fusion(bf16[1024,8192]{1,0:T(8,128)(2,1)} %copy-done.2, bf16[256,1024]{1,0:T(8,128)(2,1)S(1)} %copy-done), kind=kOutput, calls=%fused_computation.1 | convolution fusion | flops 4294967296 | bytes 25690112 | tf_op jit(solution)/shard_map/dot_general | solution.py:25
  414.3 9.0 %copy.9 = f32[256,8192]{1,0:T(8,128)} copy(f32[256,8192]{0,1:T(8,128)} %convolution_bitcast_fusion) | data formatting | bytes 16777216
  423.3 0.0 reduce-scatter.7.cloned.1.call-update
  423.3 0.1 reduce-scatter.5.cloned.1.call-done
  423.4 153.5 %reduce-scatter.7.cloned.1.call-done = f32[32,8192]{1,0:T(8,128)} async-done(((f32[256,8192]{1,0:T(8,128)}), f32[32,8192]{1,0:T(8,128)}) %reduce-scatter.7.cloned.1.call-update) | async-done | bytes 1048592
Async XLA Ops:
  7.2 393.1 %copy-start = (bf16[256,1024]{1,0:T(8,128)(2,1)S(1)}, bf16[256,1024]{1,0:T(8,128)(2,1)}, u32[]{:S(2)}) copy-start(bf16[256,1024]{1,0:T(8,128)(2,1)} %param.9) | copy-start | bytes 1572868
  7.2 28.0 %all-gather.3.cloned.1.call-start = ((), (), s32[]{:S(2)}) async-start(), calls=%async_computation.2 | async-start | bytes 2621440 | tf_op jit(solution)/shard_map/all_gather | solution.py:9
  7.9 257.0 %all-gather.5.cloned.1.call-start = ((), (), s32[]{:S(2)}) async-start(), calls=%async_computation.3 | async-start | bytes 18874368 | tf_op jit(solution)/shard_map/all_gather | solution.py:13
  8.7 414.8 %reduce-scatter.5.cloned.1.call-start = ((), (), s32[]{:S(2)}) async-start(), calls=%async_computation.4 | async-start | bytes 1310720 | tf_op jit(solution)/shard_map/reduce_scatter | solution.py:18
  264.9 129.7 %copy-start.1 = (bf16[8192,256]{1,0:T(8,128)(2,1)S(1)}, bf16[8192,256]{1,0:T(8,128)(2,1)}, u32[]{:S(2)}) copy-start(bf16[8192,256]{1,0:T(8,128)(2,1)} %param.8) | copy-start | bytes 12582916
  388.9 5.7 copy-start.2
  400.2 176.8 %reduce-scatter.7.cloned.1.call-start = ((), (), s32[]{:S(2)}) async-start(), calls=%async_computation.5 | async-start | bytes 9437184
Sparse Core Ops, SparseCore 0:
  9.6 25.5 all-gather.2
  37.3 227.5 all-gather.4
  400.3 23.0 reduce-scatter.4
  427.9 149.0 reduce-scatter.6
where the time goes:
time: 584 us
  waiting for transfers between devices  411 us (70%)
  matrix products  144 us (25%)
  local copies, waits for them, and re-layouts  14.7 us (3%)
  between operations  13.8 us (2%)
    all_gather x1, waiting for transfers between devices, on_device(): lax.all_gather(freqs, 'dp', axis=0, tiled=True)  230 us
    unnamed x5, waiting for transfers between devices  155 us
    dot_general x1, matrix products, on_device(): jnp.dot(gathered, lax.all_gather(freqs, 'dp', axis=0, tiled=True), prefer...  124 us
    all_gather x1, waiting for transfers between devices, on_device(): gathered = lax.all_gather(samples, 'feat', axis=1, tiled=True)  26.4 us
    unnamed x7, local copies, waits for them, and re-layouts  14.7 us
    dot_general x1, matrix products, on_device(): jnp.dot(corange_test, features, preferred_element_type=jnp.float32)  14.1 us
  transfers between devices with their start and end apart: 4, of which 4 were waited for; matrix products, arithmetic and copies ran while one was open for 4% of the time, Pallas kernels for 0%

commit v1 on v0

--- a/solution.py
+++ b/solution.py
@@ -6,7 +6,12 @@
 
 
 def on_device(samples, freqs, phases, range_test, corange_test):
-    gathered = lax.all_gather(samples, "feat", axis=1, tiled=True)
+    ring = [samples]
+    for hop in range(3):
+        ring.append(lax.ppermute(ring[-1], "feat", [(dev, (dev + 1) % 4) for dev in range(4)]))
+    gathered = jnp.roll(
+        jnp.concatenate(ring[::-1], axis=1), (lax.axis_index("feat") + 1) * ring[0].shape[1], axis=1
+    )
     feature_count = freqs.shape[1]
     projection = jnp.dot(
         gathered,

time: 584 us -> 559 us (0.957)
  waiting for transfers between devices: 411 us -> 379 us
  local copies, waits for them, and re-layouts: 14.7 us -> 21.7 us
    all_gather x1, waiting for transfers between devices: 230 us -> 199 us  [on_device(): lax.all_gather(freqs, 'dp', axis=0, tiled=True)]
    all_gather x1 -> x0, waiting for transfers between devices: 26.4 us -> none  [on_device(): gathered = lax.all_gather(samples, 'feat', axis=1, tiled=True)]
    ppermute x0 -> x3, waiting for transfers between devices: none -> 26.2 us  [on_device(): lax.ppermute(ring[-1], 'feat', [(dev, (dev + 1) % 4) for dev in range(4)])]
    unnamed x7 -> x18, local copies, waits for them, and re-layouts: 14.7 us -> 20.8 us
    unnamed x5 -> x4, waiting for transfers between devices: 155 us -> 154 us
  transfers between devices with their start and end apart: 4 -> 6, of which waited for: 4 -> 6; matrix products, arithmetic and copies ran while one was open for 4% -> 5% of each run, Pallas kernels for 0% -> 0%
where the time goes in v1:
time: 559 us
  waiting for transfers between devices  379 us (68%)
  matrix products  144 us (26%)
  local copies, waits for them, and re-layouts  21.7 us (4%)
  between operations  13.8 us (2%)
    all_gather x1, waiting for transfers between devices, on_device(): lax.all_gather(freqs, 'dp', axis=0, tiled=True)  199 us
    unnamed x4, waiting for transfers between devices  154 us
    dot_general x1, matrix products, on_device(): jnp.dot(gathered, lax.all_gather(freqs, 'dp', axis=0, tiled=True), prefer...  124 us
    ppermute x3, waiting for transfers between devices, on_device(): lax.ppermute(ring[-1], 'feat', [(dev, (dev + 1) % 4) for dev in range(4)])  26.2 us
    unnamed x18, local copies, waits for them, and re-layouts  20.8 us
    dot_general x1, matrix products, on_device(): jnp.dot(corange_test, features, preferred_element_type=jnp.float32)  14.1 us
  transfers between devices with their start and end apart: 6, of which 6 were waited for; matrix products, arithmetic and copies ran while one was open for 5% of the time, Pallas kernels for 0%

profile of v1, /device:TPU:0, one launch (start us, length us, event | category | flops | bytes accessed | tf_op | source)
XLA Modules:
  0.0 559.2 jit_solution(17624162532017299338)
XLA Ops:
  7.2 0.0 copy-start
  7.2 0.0 copy-start.1
  7.2 0.0 all-gather.2.cloned.1.call-start
  7.2 0.7 all-gather.2.cloned.1.call-update
  7.9 0.0 reduce-scatter.5.cloned.1.call-start
  8.0 0.5 collective-permute-start
  8.5 9.0 %collective-permute-done = bf16[1024,256]{1,0:T(8,128)(2,1)S(1)} collective-permute-done((bf16[1024,256]{1,0:T(8,128)(2,1)}, bf16[1024,256]{1,0:T(8,128)(2,1)S(1)}, u32[]{:S(2)}, u32[]{:S(2)}) %collective-permute-start) | collective-permute-done | bytes 524320 | tf_op jit(solution)/shard_map/ppermute | solution.py:11
  17.5 0.0 collective-permute-start.1
  17.5 8.6 %collective-permute-done.1 = bf16[1024,256]{1,0:T(8,128)(2,1)S(1)} collective-permute-done((bf16[1024,256]{1,0:T(8,128)(2,1)S(1)}, bf16[1024,256]{1,0:T(8,128)(2,1)S(1)}, u32[]{:S(2)}, u32[]{:S(2)}) %collective-permute-start.1) | collective-permute-done | bytes 524320 | tf_op jit(solution)/shard_map/ppermute | solution.py:11
  26.1 0.0 collective-permute-start.2
  26.1 8.6 %collective-permute-done.2 = bf16[1024,256]{1,0:T(8,128)(2,1)S(1)} collective-permute-done((bf16[1024,256]{1,0:T(8,128)(2,1)S(1)}, bf16[1024,256]{1,0:T(8,128)(2,1)S(1)}, u32[]{:S(2)}, u32[]{:S(2)}) %collective-permute-start.2) | collective-permute-done | bytes 524320 | tf_op jit(solution)/shard_map/ppermute | solution.py:11
  34.7 0.9 constant_dynamic-update-slice_fusion.7
  35.6 0.9 constant_dynamic-update-slice_fusion.6
  36.4 0.9 constant_dynamic-update-slice_fusion.5
  37.3 0.9 constant_dynamic-update-slice_fusion.4
  38.2 0.9 constant_dynamic-update-slice_fusion.3
  39.1 0.9 constant_dynamic-update-slice_fusion.2
  40.0 0.9 constant_dynamic-update-slice_fusion.1
  40.8 0.9 constant_dynamic-update-slice_fusion
  41.7 198.8 %all-gather.2.cloned.1.call-done = bf16[1024,8192]{1,0:T(8,128)(2,1)} async-done(((bf16[128,8192]{1,0:T(8,128)(2,1)}), bf16[1024,8192]{1,0:T(8,128)(2,1)}) %all-gather.2.cloned.1.call-update) | async-done | bytes 16777232 | tf_op jit(solution)/shard_map/all_gather | solution.py:18
  240.5 0.0 copy-done.3
  240.5 123.9 %multiply_convert_fusion = bf16[1024,8192]{1,0:T(8,128)(2,1)S(1)} fusion(bf16[1024,8192]{1,0:T(8,128)(2,1)} %all-gather.2.cloned.1.call-done, f32[8192]{0:T(1024)S(1)} %copy-done.3, bf16[1024,2048]{1,0:T(8,128)(2,1)} %constant_dynamic-update-slice_fusion, s32[]{:T(128)S(6)} %select_n.14), kind=kOutput, calls=%fused_computation | convolution fusion | flops 17205035008 | bytes 35684356 | tf_op jit(solution)/shard_map/dot_general | solution.py:16
  364.4 5.7 %copy-done.4 = bf16[1024,8192]{1,0:T(8,128)(2,1)} copy-done((bf16[1024,8192]{1,0:T(8,128)(2,1)}, bf16[1024,8192]{1,0:T(8,128)(2,1)S(1)}, u32[]{:S(2)}) %copy-start.4) | copy-done | bytes 16777240
  370.1 0.0 copy-done.2
  370.1 5.6 fusion.2
  375.7 0.0 reduce-scatter.5.cloned.1.call-update
  375.7 0.0 reduce-scatter.7.cloned.1.call-start
  375.8 14.1 %convolution_bitcast_fusion = f32[256,8192]{0,1:T(8,128)} fusion(bf16[1024,8192]{1,0:T(8,128)(2,1)} %copy-done.4, bf16[256,1024]{1,0:T(8,128)(2,1)S(1)} %copy-done), kind=kOutput, calls=%fused_computation.1 | convolution fusion | flops 4294967296 | bytes 25690112 | tf_op jit(solution)/shard_map/dot_general | solution.py:30
  389.9 9.0 %copy.9 = f32[256,8192]{1,0:T(8,128)} copy(f32[256,8192]{0,1:T(8,128)} %convolution_bitcast_fusion) | data formatting | bytes 16777216
  398.8 0.0 reduce-scatter.7.cloned.1.call-update
  398.8 0.1 reduce-scatter.5.cloned.1.call-done
  398.9 153.7 %reduce-scatter.7.cloned.1.call-done = f32[32,8192]{1,0:T(8,128)} async-done(((f32[256,8192]{1,0:T(8,128)}), f32[32,8192]{1,0:T(8,128)}) %reduce-scatter.7.cloned.1.call-update) | async-done | bytes 1048592
  (5 shorter events, 0.0 us)
Async XLA Ops:
  7.2 368.6 %copy-start = (bf16[256,1024]{1,0:T(8,128)(2,1)S(1)}, bf16[256,1024]{1,0:T(8,128)(2,1)}, u32[]{:S(2)}) copy-start(bf16[256,1024]{1,0:T(8,128)(2,1)} %param.9) | copy-start | bytes 1572868
  7.2 30.1 %copy-start.1 = (bf16[1024,256]{1,0:T(8,128)(2,1)S(1)}, bf16[1024,256]{1,0:T(8,128)(2,1)}, u32[]{:S(2)}) copy-start(bf16[1024,256]{1,0:T(8,128)(2,1)} %param.5) | copy-start | bytes 1572868
  7.2 233.3 %all-gather.2.cloned.1.call-start = ((), (), s32[]{:S(2)}) async-start(), calls=%async_computation.2 | async-start | bytes 18874368 | tf_op jit(solution)/shard_map/all_gather | solution.py:18
  7.9 391.0 %reduce-scatter.5.cloned.1.call-start = ((), (), s32[]{:S(2)}) async-start(), calls=%async_computation.3 | async-start | bytes 1310720 | tf_op jit(solution)/shard_map/reduce_scatter | solution.py:23
  8.0 9.5 %collective-permute-start = (bf16[1024,256]{1,0:T(8,128)(2,1)}, bf16[1024,256]{1,0:T(8,128)(2,1)S(1)}, u32[]{:S(2)}, u32[]{:S(2)}) collective-permute-start(bf16[1024,256]{1,0:T(8,128)(2,1)} %param.5), channel_id=1, source_target_pairs={{0,1},{1,2},{2,3},{3,0},{4,5},{5,6},{6,7},{7,4},{8,9},{9,10},{10,1... | collective-permute-start | bytes 1572872 | tf_op jit(solution)/shard_map/ppermute | solution.py:11
  17.5 8.6 %collective-permute-start.1 = (bf16[1024,256]{1,0:T(8,128)(2,1)S(1)}, bf16[1024,256]{1,0:T(8,128)(2,1)S(1)}, u32[]{:S(2)}, u32[]{:S(2)}) collective-permute-start(bf16[1024,256]{1,0:T(8,128)(2,1)S(1)} %collective-permute-done), channel_id=1, source_target_pairs={{0,1},{1,2},{2,3},{3,0},{4,5},{5,6},{6,7},{7,4},{8,9},{9,10},{10,1... | collective-permute-start | bytes 1572872 | tf_op jit(solution)/shard_map/ppermute | solution.py:11
  26.1 8.6 %collective-permute-start.2 = (bf16[1024,256]{1,0:T(8,128)(2,1)S(1)}, bf16[1024,256]{1,0:T(8,128)(2,1)S(1)}, u32[]{:S(2)}, u32[]{:S(2)}) collective-permute-start(bf16[1024,256]{1,0:T(8,128)(2,1)S(1)} %collective-permute-done.1), channel_id=1, source_target_pairs={{0,1},{1,2},{2,3},{3,0},{4,5},{5,6},{6,7},{7,4},{8,9},{9,10},{10,1... | collective-permute-start | bytes 1572872 | tf_op jit(solution)/shard_map/ppermute | solution.py:11
  26.1 214.4 %copy-start.3 = (f32[8192]{0:T(1024)S(1)}, f32[8192]{0:T(1024)}, u32[]{:S(2)}) copy-start(f32[8192]{0:T(1024)} %param.7) | copy-start | bytes 98308
  240.5 129.7 %copy-start.2 = (bf16[8192,256]{1,0:T(8,128)(2,1)S(1)}, bf16[8192,256]{1,0:T(8,128)(2,1)}, u32[]{:S(2)}) copy-start(bf16[8192,256]{1,0:T(8,128)(2,1)} %param.8) | copy-start | bytes 12582916
  364.4 5.7 %copy-start.4 = (bf16[1024,8192]{1,0:T(8,128)(2,1)}, bf16[1024,8192]{1,0:T(8,128)(2,1)S(1)}, u32[]{:S(2)}) copy-start(bf16[1024,8192]{1,0:T(8,128)(2,1)S(1)} %multiply_convert_fusion) | copy-start | bytes 50331652
  375.7 176.9 %reduce-scatter.7.cloned.1.call-start = ((), (), s32[]{:S(2)}) async-start(), calls=%async_computation.4 | async-start | bytes 9437184
Sparse Core Ops, SparseCore 0:
  10.1 230.2 all-gather.1
  375.8 23.0 reduce-scatter.4
  403.6 149.0 reduce-scatter.6
